TPU v7x, 32 devices: a whole 2x2x4 slice. The times are simulated.
32 devices in a mesh: cell: 16 (over z, y, x), col: 2 (over core).
Axes of the slice: x: 2, y: 2, z: 4, core: 2. Of those that a mesh axis runs over, the one named last changes fastest.
Arguments:
- panel_block: float32 [8192, 512], P('cell', 'col'), may hold values from -0.176776695 to 0.176776695, as said below
- trailing: float32 [8192, 1792], P('cell', 'col'), may hold values from -6 to 6
Outputs:
- triangle: float32 [512, 512], replicated
- coupling: float32 [512, 1792], P('cell', 'col')
- projected: float32 [8192, 1792], P('cell', 'col')
Inputs may be any that keep to these rules, and one draw needn't show every extreme that they name: `panel_block`: the panel has full column rank.
All inputs are finite; a program needn't handle non-finite values.
Results may differ from a plain program's by a relative error of at most 0.0003.
Values sent between devices are 32-bit elements; how exact they have to be, the bound alone decides.
A program may use at most 64 MiB of HBM per device.

v0:
```python
import functools

import jax
import jax.numpy as jnp
from jax import lax
from jax.experimental import pallas as pl
from jax.experimental.pallas import tpu as pltpu
from jax.sharding import PartitionSpec as P

MESH = pl.DeviceIdType.MESH
TILE = 128
PIVOTS = 8


def split2(x):
    high = x.astype(jnp.bfloat16)
    low = (x - high.astype(jnp.float32)).astype(jnp.bfloat16)
    return high, low


def split3(x):
    a = x.astype(jnp.bfloat16).astype(jnp.float32)
    rest = x - a
    b = rest.astype(jnp.bfloat16).astype(jnp.float32)
    c = (rest - b).astype(jnp.bfloat16).astype(jnp.float32)
    return a, b, c


def dot(a, b, dims=((1,), (0,))):
    return lax.dot_general(a, b, (dims, ((), ())), preferred_element_type=jnp.float32)


def dot3(a, b_high, b_low, dims=((1,), (0,))):
    a_high, a_low = split2(a)
    return dot(a_high, b_high, dims) + (dot(a_high, b_low, dims) + dot(a_low, b_high, dims))


def small_factor(corner):
    n = PIVOTS
    full = (n, TILE)
    a = {}
    for j in range(n):
        column = jnp.broadcast_to(corner[:, j : j + 1], full)
        for i in range(j, n):
            a[i, j] = jnp.broadcast_to(column[i : i + 1, :], full)
    low, inv, m = {}, {}, {}
    for j in range(n):
        y = lax.rsqrt(a[j, j])
        inv[j] = y * (1.5 - (0.5 * a[j, j]) * (y * y))
        for i in range(j + 1, n):
            low[i, j] = a[i, j] * inv[j]
        for i in range(j + 1, n):
            for p in range(j + 1, i + 1):
                a[i, p] = a[i, p] - low[i, j] * low[p, j]
        m[j, j] = inv[j]
        for p in range(j):
            total = low[j, p] * m[p, p]
            for q in range(p + 1, j):
                total = total + low[j, q] * m[q, p]
            m[j, p] = -inv[j] * total
    sublane = lax.broadcasted_iota(jnp.int32, full, 0)
    columns = []
    for j in range(n):
        column = jnp.zeros(full, jnp.float32)
        for i in range(j, n):
            column = jnp.where(sublane == i, m[i, j], column)
        columns.append(column)
    return columns


def eliminate_block(x_ref, k):
    size = x_ref.shape[0]
    base = k * TILE
    window = slice(base, base + size + TILE)
    width = size + TILE
    lane = lax.broadcasted_iota(jnp.int32, (PIVOTS, TILE), 1)

    def step(b, carry):
        first = pl.multiple_of(base + b * PIVOTS, PIVOTS)
        rows = x_ref[pl.ds(first, PIVOTS), window]
        corner = pltpu.roll(rows[:, :TILE], lax.rem(TILE - b * PIVOTS, TILE), 1)
        columns = small_factor(corner)
        done = None
        for j in range(PIVOTS):
            spread = jnp.concatenate([columns[j]] * (width // TILE), axis=1)
            term = spread * jnp.broadcast_to(rows[j : j + 1, :], (PIVOTS, width))
            done = term if done is None else done + term
        a, bb, c = split3(done)
        below = lane >= (b + 1) * PIVOTS
        la, lb, lc = (jnp.where(below, part[:, :TILE], 0.0) for part in (a, bb, c))
        left = jnp.concatenate([la, la, lb, la, lc, lb], axis=0).astype(jnp.bfloat16)
        right = jnp.concatenate([a, bb, a, c, a, bb], axis=0).astype(jnp.bfloat16)
        change = dot(left, right, ((0,), (0,)))
        x_ref[base : base + TILE, window] = x_ref[base : base + TILE, window] - change
        x_ref[pl.ds(first, PIVOTS), window] = done
        return carry

    lax.fori_loop(0, TILE // PIVOTS, step, 0)
    for r in range(k + 1, size // TILE):
        left = x_ref[base : base + TILE, r * TILE : (r + 1) * TILE]
        change = lax.dot_general(
            left,
            x_ref[base : base + TILE, window],
            (((0,), (0,)), ((), ())),
            precision=lax.Precision.HIGHEST,
            preferred_element_type=jnp.float32,
        )
        x_ref[r * TILE : (r + 1) * TILE, window] = (
            x_ref[r * TILE : (r + 1) * TILE, window] - change
        )


class Summed:
    def __init__(self, part, full_at, near, acc, far, send, recv, groups, place):
        self.part, self.full_at = part, full_at
        self.near, self.acc, self.far = near, acc, far
        self.send, self.recv = send, recv
        self.inner, self.outer = groups
        self.hi, self.lo, self.col = place
        self.big = part.shape[0] // self.inner
        self.small = self.big // self.outer
        self.copies = [[], [], [], []]

    def start(self, phase, d, src, dst, device):
        copy = pltpu.make_async_remote_copy(
            src_ref=src,
            dst_ref=dst,
            send_sem=self.send.at[phase, d - 1],
            recv_sem=self.recv.at[phase, d - 1],
            device_id=(device, self.col),
            device_id_type=MESH,
        )
        copy.start()
        self.copies[phase].append(copy)

    def rows(self, index, size):
        return pl.ds(pl.multiple_of(index * size, size), size)

    def arrived(self, phase):
        for copy in self.copies[phase]:
            copy.wait_recv()

    def begin(self):
        for d in range(1, self.inner):
            other = lax.rem(self.lo + d, self.inner)
            self.start(0, d, self.part.at[self.rows(other, self.big)], self.near.at[d - 1], self.hi * self.inner + other)

    def second(self):
        self.arrived(0)
        total = self.part[self.rows(self.lo, self.big), :]
        for d in range(self.inner - 1):
            total = total + self.near[d]
        self.acc[...] = total
        for d in range(1, self.outer):
            other = lax.rem(self.hi + d, self.outer)
            self.start(1, d, self.acc.at[self.rows(other, self.small)], self.far.at[d - 1], other * self.inner + self.lo)

    def third(self):
        self.arrived(1)
        total = self.acc[self.rows(self.hi, self.small), :]
        for d in range(self.outer - 1):
            total = total + self.far[d]
        mine = self.full_at(self.rows(self.lo * self.outer + self.hi, self.small))
        mine[...] = total
        for d in range(1, self.outer):
            other = lax.rem(self.hi + d, self.outer)
            self.start(2, d, mine, mine, other * self.inner + self.lo)

    def fourth(self):
        self.arrived(2)
        mine = self.full_at(self.rows(self.lo, self.big))
        for d in range(1, self.inner):
            other = lax.rem(self.lo + d, self.inner)
            self.start(3, d, mine, mine, self.hi * self.inner + other)

    def finish(self):
        self.arrived(3)

    def drain(self):
        for phase in self.copies:
            for copy in phase:
                copy.wait_send()


def kernel(
    cells, cols, inner,
    panel_ref, trail_ref, tri_ref, coup_ref, proj_ref,
    parts, panel, panel_t, gram_part, grams, x, high, low, inv_high, inv_low, basis,
    cross_part, cross, coupling,
    g_near, g_acc, g_far, c_near, c_acc, c_far,
    col_send, col_recv, g_send, g_recv, c_send, c_recv,
):
    outer = cells // inner
    me, col = lax.axis_index("cell"), lax.axis_index("col")
    hi, lo = lax.div(me, inner), lax.rem(me, inner)
    rows, own = panel_ref.shape
    size = x.shape[0]
    tiles = size // TILE

    barrier = pltpu.get_barrier_semaphore()
    for d in range(1, inner):
        pl.semaphore_signal(barrier, inc=1, device_id=(hi * inner + lax.rem(lo + d, inner), col), device_id_type=MESH)
    for d in range(1, outer):
        pl.semaphore_signal(barrier, inc=1, device_id=(lax.rem(hi + d, outer) * inner + lo, col), device_id_type=MESH)
    for d in range(1, cols):
        pl.semaphore_signal(barrier, inc=1, device_id=(me, lax.rem(col + d, cols)), device_id_type=MESH)
    pl.semaphore_wait(barrier, inner + outer + cols - 3)

    def share(phase, src, dst):
        copies = []
        for d in range(1, cols):
            copy = pltpu.make_async_remote_copy(
                src_ref=src,
                dst_ref=dst,
                send_sem=col_send.at[phase, d - 1],
                recv_sem=col_recv.at[phase, d - 1],
                device_id=(me, lax.rem(col + d, cols)),
                device_id_type=MESH,
            )
            copy.start()
            copies.append(copy)
        return copies

    panel_copies = share(0, panel_ref, parts.at[col])
    parts[col] = panel_ref[...]
    t_high, t_low = split2(trail_ref[...])
    high[...] = t_high
    low[...] = t_low
    for copy in panel_copies:
        copy.wait_recv()
    for c in range(cols):
        panel[:, c * own : (c + 1) * own] = parts[c]

    @pl.loop(0, tiles)
    def _(i):
        at = pl.ds(pl.multiple_of(i * TILE, TILE), TILE)
        turned = jnp.transpose(panel[:, at])
        panel_t[at, :] = turned
        gram_part[at, :] = lax.dot_general(
            turned,
            panel_ref[...],
            (((1,), (0,)), ((), ())),
            precision=lax.Precision.HIGHEST,
            preferred_element_type=jnp.float32,
        )

    groups, place = (inner, outer), (hi, lo, col)
    gram_sum = Summed(gram_part, lambda r: grams.at[col, r, :], g_near, g_acc, g_far, g_send, g_recv, groups, place)
    cross_sum = Summed(cross_part, lambda r: cross.at[r, :], c_near, c_acc, c_far, c_send, c_recv, groups, place)
    gram_sum.begin()

    @pl.loop(0, tiles)
    def _(i):
        at = pl.ds(pl.multiple_of(i * TILE, TILE), TILE)
        cross_part[at, :] = dot3(panel_t[at, :], high[...], low[...])

    gram_sum.second()
    gram_sum.third()
    cross_sum.begin()
    gram_sum.fourth()
    row = lax.broadcasted_iota(jnp.int32, (size, size), 0)
    column = lax.broadcasted_iota(jnp.int32, (size, size), 1)
    x[:, size:] = jnp.where(row == column, 1.0, 0.0)
    gram_sum.finish()
    gram_copies = share(1, grams.at[col], grams.at[col])
    for copy in gram_copies:
        copy.wait_recv()
    for c in range(cols):
        x[:, c * own : (c + 1) * own] = grams[c]

    later = [cross_sum.second, cross_sum.third, cross_sum.fourth]
    for k in range(tiles):
        eliminate_block(x, k)
        if later:
            later.pop(0)()
    for call in later:
        call()

    tri_ref[...] = jnp.where(row <= column, x[:, :size], 0.0)
    m_high, m_low = split2(x[:, size:])
    inv_high[...] = m_high
    inv_low[...] = m_low

    @pl.loop(0, rows // TILE)
    def _(i):
        at = pl.ds(pl.multiple_of(i * TILE, TILE), TILE)
        basis[at, :] = dot3(panel[at, :], inv_high[...], inv_low[...], ((1,), (1,)))

    cross_sum.finish()
    c_high, c_low = split2(cross[...])
    high[:size] = c_high
    low[:size] = c_low

    @pl.loop(0, tiles)
    def _(i):
        at = pl.ds(pl.multiple_of(i * TILE, TILE), TILE)
        coupling[at, :] = dot3(x[at, size:], high[:size], low[:size])

    share_rows = size // cells
    coup_ref[...] = coupling[pl.ds(pl.multiple_of(me * share_rows, share_rows), share_rows), :]
    k_high, k_low = split2(coupling[...])
    high[:size] = k_high
    low[:size] = k_low

    @pl.loop(0, rows // TILE)
    def _(i):
        at = pl.ds(pl.multiple_of(i * TILE, TILE), TILE)
        proj_ref[at, :] = trail_ref[at, :] - dot3(basis[at, :], high[:size], low[:size])

    for copy in panel_copies + gram_copies:
        copy.wait_send()
    gram_sum.drain()
    cross_sum.drain()


def on_device(cells, cols, panel_block, trailing):
    rows, own = panel_block.shape
    size = own * cols
    wide = trailing.shape[1]
    inner = 1
    while inner * inner < cells:
        inner *= 2
    outer = cells // inner
    big, small = size // inner, size // cells
    tall = max(rows, size)
    f32, bf16 = jnp.float32, jnp.bfloat16
    vmem = pl.BlockSpec(memory_space=pltpu.VMEM)

    def stages(width):
        return [
            pltpu.VMEM((inner - 1, big, width), f32),
            pltpu.VMEM((big, width), f32),
            pltpu.VMEM((outer - 1, small, width), f32),
        ]

    peers = max(inner, outer) - 1
    triangle, coupling, projected = pl.pallas_call(
        functools.partial(kernel, cells, cols, inner),
        out_shape=[
            jax.ShapeDtypeStruct((size, size), f32),
            jax.ShapeDtypeStruct((small, wide), f32),
            jax.ShapeDtypeStruct((rows, wide), f32),
        ],
        in_specs=[vmem] * 2,
        out_specs=[vmem] * 3,
        scratch_shapes=[
            pltpu.VMEM((cols, rows, own), f32),
            pltpu.VMEM((rows, size), f32),
            pltpu.VMEM((size, rows), f32),
            pltpu.VMEM((size, own), f32),
            pltpu.VMEM((cols, size, own), f32),
            pltpu.VMEM((size, 2 * size), f32),
            pltpu.VMEM((tall, wide), bf16),
            pltpu.VMEM((tall, wide), bf16),
            pltpu.VMEM((size, size), bf16),
            pltpu.VMEM((size, size), bf16),
            pltpu.VMEM((rows, size), f32),
            pltpu.VMEM((size, wide), f32),
            pltpu.VMEM((size, wide), f32),
            pltpu.VMEM((size, wide), f32),
        ]
        + stages(own)
        + stages(wide)
        + [pltpu.SemaphoreType.DMA((2, cols - 1))] * 2
        + [pltpu.SemaphoreType.DMA((4, peers))] * 4,
        compiler_params=pltpu.CompilerParams(
            collective_id=0, has_side_effects=True, vmem_limit_bytes=56 * 2**20
        ),
    )(panel_block, trailing)
    return triangle, coupling, projected


def solution(mesh):
    placed = (P("cell", "col"), P("cell", "col"))
    return jax.shard_map(
        functools.partial(on_device, mesh.shape["cell"], mesh.shape["col"]),
        mesh=mesh,
        in_specs=placed,
        out_specs=(P(), P("cell", "col"), P("cell", "col")),
        check_vma=False,
    )
```

profile of v0, /device:TPU:1, one launch (start us, length us, event | category | flops | bytes accessed | tf_op | source)
XLA Modules:
  0.0 112.8 jit_solution(10059187242677809237)
XLA Ops:
  0.6 107.8 %shard_map.49 = (f32[512,512]{1,0:T(8,128)}, f32[32,896]{1,0:T(8,128)}, f32[512,896]{1,0:T(8,128)}) custom-call(f32[512,256]{1,0:T(8,128)} %panel_ref.1, f32[512,896]{1,0:T(8,128)} %trail_ref.1), custom_call_target="tpu_custom_call" | custom-call | tf_op jit(solution)/shard_map/pallas_call | solution.py:337
  108.5 0.0 copy-start.1
  108.5 0.0 copy-start
  108.5 2.4 %copy.8 = f32[512,512]{1,0:T(8,128)} copy(f32[512,512]{1,0:T(8,128)} %get-tuple-element.6) | data formatting | bytes 2097152
  110.9 0.0 copy-done.1
  110.9 0.6 copy.9
  111.6 0.0 copy-done
  111.6 1.2 %copy.10 = f32[512,896]{1,0:T(8,128)} copy(f32[512,896]{1,0:T(8,128)S(1)} %copy-done) | data formatting | bytes 3670016
Async XLA Ops:
  108.5 2.4 %copy-start.1 = (f32[32,896]{1,0:T(8,128)S(1)}, f32[32,896]{1,0:T(8,128)}, u32[]{:S(2)}) copy-start(f32[32,896]{1,0:T(8,128)} %get-tuple-element.7) | copy-start | bytes 344068
  108.5 3.1 %copy-start = (f32[512,896]{1,0:T(8,128)S(1)}, f32[512,896]{1,0:T(8,128)}, u32[]{:S(2)}) copy-start(f32[512,896]{1,0:T(8,128)} %get-tuple-element.8) | copy-start | bytes 5505028
where the time goes:
time: 115 us; the launch traced here: 113 us
  Pallas kernels  108 us (94%)
  local copies, waits for them, and re-layouts  4.28 us (4%)
    pallas_call x1, Pallas kernels, on_device(): pl.pallas_call(functools.partial(kernel, cells, cols, inner), out_shape=[...  108 us
    unnamed x7, local copies, waits for them, and re-layouts  4.28 us

commit v1 on v0

--- a/solution.py
+++ b/solution.py
@@ -68,7 +68,7 @@
     return columns
 
 
-def eliminate_block(x_ref, k):
+def eliminate_rows(x_ref, k, start, stop):
     size = x_ref.shape[0]
     base = k * TILE
     window = slice(base, base + size + TILE)
@@ -95,7 +95,13 @@
         x_ref[pl.ds(first, PIVOTS), window] = done
         return carry
 
-    lax.fori_loop(0, TILE // PIVOTS, step, 0)
+    lax.fori_loop(start, stop, step, 0)
+
+
+def update_below(x_ref, k):
+    size = x_ref.shape[0]
+    base = k * TILE
+    window = slice(base, base + size + TILE)
     for r in range(k + 1, size // TILE):
         left = x_ref[base : base + TILE, r * TILE : (r + 1) * TILE]
         change = lax.dot_general(
@@ -111,23 +117,24 @@
 
 
 class Summed:
-    def __init__(self, part, full_at, near, acc, far, send, recv, groups, place):
-        self.part, self.full_at = part, full_at
-        self.near, self.acc, self.far = near, acc, far
+    def __init__(self, part_at, full_at, scratch, send, recv, counts, place, device, size):
+        self.part_at, self.full_at = part_at, full_at
+        self.near, self.acc, self.far = scratch
         self.send, self.recv = send, recv
-        self.inner, self.outer = groups
-        self.hi, self.lo, self.col = place
-        self.big = part.shape[0] // self.inner
-        self.small = self.big // self.outer
+        self.nears, self.fars = counts
+        self.n, self.f = place
+        self.device = device
+        self.big = size // self.nears
+        self.small = self.big // self.fars
         self.copies = [[], [], [], []]
 
-    def start(self, phase, d, src, dst, device):
+    def start(self, phase, d, src, dst, device_id):
         copy = pltpu.make_async_remote_copy(
             src_ref=src,
             dst_ref=dst,
             send_sem=self.send.at[phase, d - 1],
             recv_sem=self.recv.at[phase, d - 1],
-            device_id=(device, self.col),
+            device_id=device_id,
             device_id_type=MESH,
         )
         copy.start()
@@ -141,37 +148,37 @@
             copy.wait_recv()
 
     def begin(self):
-        for d in range(1, self.inner):
-            other = lax.rem(self.lo + d, self.inner)
-            self.start(0, d, self.part.at[self.rows(other, self.big)], self.near.at[d - 1], self.hi * self.inner + other)
+        for d in range(1, self.nears):
+            other = lax.rem(self.n + d, self.nears)
+            self.start(0, d, self.part_at(self.rows(other, self.big)), self.near.at[d - 1], self.device(other, self.f))
 
     def second(self):
         self.arrived(0)
-        total = self.part[self.rows(self.lo, self.big), :]
-        for d in range(self.inner - 1):
+        total = self.part_at(self.rows(self.n, self.big))[...]
+        for d in range(self.nears - 1):
             total = total + self.near[d]
         self.acc[...] = total
-        for d in range(1, self.outer):
-            other = lax.rem(self.hi + d, self.outer)
-            self.start(1, d, self.acc.at[self.rows(other, self.small)], self.far.at[d - 1], other * self.inner + self.lo)
+        for d in range(1, self.fars):
+            other = lax.rem(self.f + d, self.fars)
+            self.start(1, d, self.acc.at[self.rows(other, self.small)], self.far.at[d - 1], self.device(self.n, other))
 
     def third(self):
         self.arrived(1)
-        total = self.acc[self.rows(self.hi, self.small), :]
-        for d in range(self.outer - 1):
+        total = self.acc[self.rows(self.f, self.small), :]
+        for d in range(self.fars - 1):
             total = total + self.far[d]
-        mine = self.full_at(self.rows(self.lo * self.outer + self.hi, self.small))
+        mine = self.full_at(self.rows(self.n * self.fars + self.f, self.small))
         mine[...] = total
-        for d in range(1, self.outer):
-            other = lax.rem(self.hi + d, self.outer)
-            self.start(2, d, mine, mine, other * self.inner + self.lo)
+        for d in range(1, self.fars):
+            other = lax.rem(self.f + d, self.fars)
+            self.start(2, d, mine, mine, self.device(self.n, other))
 
     def fourth(self):
         self.arrived(2)
-        mine = self.full_at(self.rows(self.lo, self.big))
-        for d in range(1, self.inner):
-            other = lax.rem(self.lo + d, self.inner)
-            self.start(3, d, mine, mine, self.hi * self.inner + other)
+        mine = self.full_at(self.rows(self.n, self.big))
+        for d in range(1, self.nears):
+            other = lax.rem(self.n + d, self.nears)
+            self.start(3, d, mine, mine, self.device(other, self.f))
 
     def finish(self):
         self.arrived(3)
@@ -187,8 +194,8 @@
     panel_ref, trail_ref, tri_ref, coup_ref, proj_ref,
     parts, panel, panel_t, gram_part, grams, x, high, low, inv_high, inv_low, basis,
     cross_part, cross, coupling,
-    g_near, g_acc, g_far, c_near, c_acc, c_far,
-    col_send, col_recv, g_send, g_recv, c_send, c_recv,
+    g_near, g_acc, g_far, a_near, a_acc, a_far, b_near, b_acc, b_far,
+    col_send, col_recv, g_send, g_recv, a_send, a_recv, b_send, b_recv,
 ):
     outer = cells // inner
     me, col = lax.axis_index("cell"), lax.axis_index("col")
@@ -244,9 +251,26 @@
             preferred_element_type=jnp.float32,
         )
 
-    groups, place = (inner, outer), (hi, lo, col)
-    gram_sum = Summed(gram_part, lambda r: grams.at[col, r, :], g_near, g_acc, g_far, g_send, g_recv, groups, place)
-    cross_sum = Summed(cross_part, lambda r: cross.at[r, :], c_near, c_acc, c_far, c_send, c_recv, groups, place)
+    cut = a_acc.shape[1]
+
+    def by_plane(near, far):
+        return far * inner + near, col
+
+    def by_line(near, far):
+        return near * inner + far, col
+
+    gram_sum = Summed(
+        lambda r: gram_part.at[r, :], lambda r: grams.at[col, r, :],
+        (g_near, g_acc, g_far), g_send, g_recv, (inner, outer), (lo, hi), by_plane, size,
+    )
+    sum_a = Summed(
+        lambda r: cross_part.at[r, :cut], lambda r: cross.at[r, :cut],
+        (a_near, a_acc, a_far), a_send, a_recv, (inner, outer), (lo, hi), by_plane, size,
+    )
+    sum_b = Summed(
+        lambda r: cross_part.at[r, cut:], lambda r: cross.at[r, cut:],
+        (b_near, b_acc, b_far), b_send, b_recv, (outer, inner), (hi, lo), by_line, size,
+    )
     gram_sum.begin()
 
     @pl.loop(0, tiles)
@@ -254,9 +278,10 @@
         at = pl.ds(pl.multiple_of(i * TILE, TILE), TILE)
         cross_part[at, :] = dot3(panel_t[at, :], high[...], low[...])
 
+    sum_a.begin()
+    sum_b.begin()
     gram_sum.second()
     gram_sum.third()
-    cross_sum.begin()
     gram_sum.fourth()
     row = lax.broadcasted_iota(jnp.int32, (size, size), 0)
     column = lax.broadcasted_iota(jnp.int32, (size, size), 1)
@@ -268,13 +293,22 @@
     for c in range(cols):
         x[:, c * own : (c + 1) * own] = grams[c]
 
-    later = [cross_sum.second, cross_sum.third, cross_sum.fourth]
+    later = {
+        1: (sum_a.second, sum_b.second),
+        3: (sum_a.third, sum_b.third),
+        5: (sum_a.fourth, sum_b.fourth),
+    }
+    half = TILE // PIVOTS // 2
     for k in range(tiles):
-        eliminate_block(x, k)
-        if later:
-            later.pop(0)()
-    for call in later:
-        call()
+        for part in range(2):
+            eliminate_rows(x, k, part * half, part * half + half)
+            if part == 1:
+                update_below(x, k)
+            for call in later.pop(2 * k + part + 1, ()):
+                call()
+    for calls in later.values():
+        for call in calls:
+            call()
 
     tri_ref[...] = jnp.where(row <= column, x[:, :size], 0.0)
     m_high, m_low = split2(x[:, size:])
@@ -286,7 +320,8 @@
         at = pl.ds(pl.multiple_of(i * TILE, TILE), TILE)
         basis[at, :] = dot3(panel[at, :], inv_high[...], inv_low[...], ((1,), (1,)))
 
-    cross_sum.finish()
+    sum_a.finish()
+    sum_b.finish()
     c_high, c_low = split2(cross[...])
     high[:size] = c_high
     low[:size] = c_low
@@ -310,7 +345,8 @@
     for copy in panel_copies + gram_copies:
         copy.wait_send()
     gram_sum.drain()
-    cross_sum.drain()
+    sum_a.drain()
+    sum_b.drain()
 
 
 def on_device(cells, cols, panel_block, trailing):
@@ -321,18 +357,19 @@
     while inner * inner < cells:
         inner *= 2
     outer = cells // inner
-    big, small = size // inner, size // cells
+    small = size // cells
     tall = max(rows, size)
     f32, bf16 = jnp.float32, jnp.bfloat16
     vmem = pl.BlockSpec(memory_space=pltpu.VMEM)
 
-    def stages(width):
+    def stages(nears, fars, width):
         return [
-            pltpu.VMEM((inner - 1, big, width), f32),
-            pltpu.VMEM((big, width), f32),
-            pltpu.VMEM((outer - 1, small, width), f32),
+            pltpu.VMEM((nears - 1, size // nears, width), f32),
+            pltpu.VMEM((size // nears, width), f32),
+            pltpu.VMEM((fars - 1, small, width), f32),
         ]
 
+    cut = wide - max(1, wide // TILE * 2 // 7) * TILE
     peers = max(inner, outer) - 1
     triangle, coupling, projected = pl.pallas_call(
         functools.partial(kernel, cells, cols, inner),
@@ -359,10 +396,11 @@
             pltpu.VMEM((size, wide), f32),
             pltpu.VMEM((size, wide), f32),
         ]
-        + stages(own)
-        + stages(wide)
+        + stages(inner, outer, own)
+        + stages(inner, outer, cut)
+        + stages(outer, inner, wide - cut)
         + [pltpu.SemaphoreType.DMA((2, cols - 1))] * 2
-        + [pltpu.SemaphoreType.DMA((4, peers))] * 4,
+        + [pltpu.SemaphoreType.DMA((4, peers))] * 6,
         compiler_params=pltpu.CompilerParams(
             collective_id=0, has_side_effects=True, vmem_limit_bytes=56 * 2**20
         ),

time: 115 us -> 92.8 us (0.81); the launches traced: 113 us -> 92.7 us
  Pallas kernels: 108 us -> 87.7 us
    pallas_call x1, Pallas kernels: 108 us -> 87.7 us  [on_device(): pl.pallas_call(functools.partial(kernel, cells, cols, inner), out_shape=[...]
where the time goes in v1:
time: 92.8 us; the launch traced here: 92.7 us
  Pallas kernels  87.7 us (95%)
  local copies, waits for them, and re-layouts  4.28 us (5%)
    pallas_call x1, Pallas kernels, on_device(): pl.pallas_call(functools.partial(kernel, cells, cols, inner), out_shape=[...  87.7 us
    unnamed x7, local copies, waits for them, and re-layouts  4.28 us

profile of v1, /device:TPU:1, one launch (start us, length us, event | category | flops | bytes accessed | tf_op | source)
XLA Modules:
  0.0 92.7 jit_solution(14131446427712364553)
XLA Ops:
  0.6 87.7 %shard_map.49 = (f32[512,512]{1,0:T(8,128)}, f32[32,896]{1,0:T(8,128)}, f32[512,896]{1,0:T(8,128)}) custom-call(f32[512,256]{1,0:T(8,128)} %panel_ref.1, f32[512,896]{1,0:T(8,128)} %trail_ref.1), custom_call_target="tpu_custom_call" | custom-call | tf_op jit(solution)/shard_map/pallas_call | solution.py:374
  88.4 0.0 copy-start.1
  88.4 0.0 copy-start
  88.4 2.4 %copy.8 = f32[512,512]{1,0:T(8,128)} copy(f32[512,512]{1,0:T(8,128)} %get-tuple-element.6) | data formatting | bytes 2097152
  90.8 0.0 copy-done.1
  90.8 0.6 copy.9
  91.4 0.0 copy-done
  91.4 1.2 %copy.10 = f32[512,896]{1,0:T(8,128)} copy(f32[512,896]{1,0:T(8,128)S(1)} %copy-done) | data formatting | bytes 3670016
Async XLA Ops:
  88.4 2.4 %copy-start.1 = (f32[32,896]{1,0:T(8,128)S(1)}, f32[32,896]{1,0:T(8,128)}, u32[]{:S(2)}) copy-start(f32[32,896]{1,0:T(8,128)} %get-tuple-element.7) | copy-start | bytes 344068
  88.4 3.1 %copy-start = (f32[512,896]{1,0:T(8,128)S(1)}, f32[512,896]{1,0:T(8,128)}, u32[]{:S(2)}) copy-start(f32[512,896]{1,0:T(8,128)} %get-tuple-element.8) | copy-start | bytes 5505028

commit v2 on v1

--- a/solution.py
+++ b/solution.py
@@ -95,7 +95,7 @@
         x_ref[pl.ds(first, PIVOTS), window] = done
         return carry
 
-    lax.fori_loop(start, stop, step, 0)
+    lax.fori_loop(start, stop, step, 0, unroll=4)
 
 
 def update_below(x_ref, k):

time: 92.8 us -> 93.3 us (level)
  no operation moved by 1% of the time
where the time goes in v2:
time: 93.3 us; the launch traced here: 93.1 us
  Pallas kernels  88.2 us (95%)
  local copies, waits for them, and re-layouts  4.28 us (5%)
    pallas_call x1, Pallas kernels, on_device(): pl.pallas_call(functools.partial(kernel, cells, cols, inner), out_shape=[...  88.2 us
    unnamed x7, local copies, waits for them, and re-layouts  4.28 us

profile of v2, /device:TPU:1, one launch (start us, length us, event | category | flops | bytes accessed | tf_op | source)
XLA Modules:
  0.0 93.1 jit_solution(17266726620669124055)
XLA Ops:
  0.6 88.2 %shard_map.49 = (f32[512,512]{1,0:T(8,128)}, f32[32,896]{1,0:T(8,128)}, f32[512,896]{1,0:T(8,128)}) custom-call(f32[512,256]{1,0:T(8,128)} %panel_ref.1, f32[512,896]{1,0:T(8,128)} %trail_ref.1), custom_call_target="tpu_custom_call" | custom-call | tf_op jit(solution)/shard_map/pallas_call | solution.py:374
  88.8 0.0 copy-start.1
  88.8 0.0 copy-start
  88.8 2.4 %copy.8 = f32[512,512]{1,0:T(8,128)} copy(f32[512,512]{1,0:T(8,128)} %get-tuple-element.6) | data formatting | bytes 2097152
  91.2 0.0 copy-done.1
  91.2 0.6 copy.9
  91.9 0.0 copy-done
  91.9 1.2 %copy.10 = f32[512,896]{1,0:T(8,128)} copy(f32[512,896]{1,0:T(8,128)S(1)} %copy-done) | data formatting | bytes 3670016
Async XLA Ops:
  88.8 2.4 %copy-start.1 = (f32[32,896]{1,0:T(8,128)S(1)}, f32[32,896]{1,0:T(8,128)}, u32[]{:S(2)}) copy-start(f32[32,896]{1,0:T(8,128)} %get-tuple-element.7) | copy-start | bytes 344068
  88.8 3.1 %copy-start = (f32[512,896]{1,0:T(8,128)S(1)}, f32[512,896]{1,0:T(8,128)}, u32[]{:S(2)}) copy-start(f32[512,896]{1,0:T(8,128)} %get-tuple-element.8) | copy-start | bytes 5505028
